TPU v7x, 512 devices: a whole 4x4x16 slice. The times are simulated.
512 devices in a mesh: agent: 16 (over x, y), dp: 32 (over z, core).
Axes of the slice: x: 4, y: 4, z: 16, core: 2. Of those that a mesh axis runs over, the one named last changes fastest.
Arguments:
- learn_obs: bfloat16 [16, 1024, 16, 3456], P('agent', 'dp'), may hold values from -6 to 6
- own_obs: bfloat16 [16, 1024, 3456], P('agent', 'dp'), may hold values from -6 to 6
- opp_obs: bfloat16 [16, 1024, 3456], P('agent', 'dp'), may hold values from -6 to 6
- opponent: int32 [16, 1024, 1], P('agent', 'dp'), may hold values from 0 to 15; in each aligned block of 32 rows (0 to 31, 32 to 63, ..., all dimensions but the last counted through in order) at most 8 rows name the same one
- actions: int32 [16, 1024, 16], P('agent', 'dp'), may hold values from 0 to 17
- done: int32 [16, 1024, 16], P('agent', 'dp'), may hold values 0 or 1
- rewards: float32 [16, 1024, 16], P('agent', 'dp'), may hold values from -6 to 6
- behaviour: float32 [16, 1024, 16], P('agent', 'dp'), may hold values from -4.5 to -1.5
- core_master: float32 [16, 256, 3712], P('agent', 'dp'), may hold values from -0.109375 to 0.109375
- core_mom: float32 [16, 256, 3712], P('agent', 'dp'), may hold values from -6 to 6
- core_vel: float32 [16, 256, 3712], P('agent', 'dp'), may hold values from 0.1 to 1
- head_master: float32 [16, 19, 256], P('agent'), may hold values from -0.375 to 0.375
- head_mom: float32 [16, 19, 256], P('agent'), may hold values from -6 to 6
- head_vel: float32 [16, 19, 256], P('agent'), may hold values from 0.1 to 1
- rates: float32 [16], P('agent'), may hold values from 0.01 to 0.1
Outputs:
- own_logits: float32 [16, 1024, 18], P('agent', 'dp')
- opp_logits: bfloat16 [16, 1024, 18], P('agent', 'dp')
- new_core: float32 [16, 256, 3712], P('agent', 'dp')
- new_core_mom: float32 [16, 256, 3712], P('agent', 'dp')
- new_core_vel: float32 [16, 256, 3712], P('agent', 'dp')
- new_head: float32 [16, 19, 256], P('agent')
- new_head_mom: float32 [16, 19, 256], P('agent')
- new_head_vel: float32 [16, 19, 256], P('agent')
Inputs may be any that keep to these rules, and one draw needn't show every extreme that they name: Among the 32 environments of one device (aligned blocks of the environment dimension), at most 8 face the same opponent agent, and some device reaches 8 in every draw.
All inputs are finite; a program needn't handle non-finite values. No bound on the sum of `done` on one device may be relied on, other than what follows from the above.
Results may differ from a plain program's by a relative error of at most 0.023.
Values may be sent and summed in bfloat16 or wider, within the bound.
A program may use at most 64 MiB of HBM per device.

v0:
```python
import jax
import jax.numpy as jnp
from jax import lax
from jax.sharding import Mesh
from jax.sharding import PartitionSpec as P

BLOCK = 128
DP = ("dp_0", "dp_1")
gamma_rate = 0.99
baseline_cost = 0.5
entropy_cost = 0.05
beta_first = 0.9
beta_second = 0.99
adam_eps = 1e-08


def joined_along(blocks, dim):
    shape = list(blocks.shape[1:])
    shape[dim] *= blocks.shape[0]
    return jnp.moveaxis(blocks, 0, dim).reshape(shape)


def stacked_from(x, axes, order):
    blocks = x[None]
    for k in order:
        blocks = lax.all_gather(blocks, axes[k], axis=0, tiled=True)
    current = [lax.axis_size(axes[k]) for k in reversed(order)]
    blocks = blocks.reshape(*current, *x.shape)
    turned = sorted(range(len(order)), key=lambda place: order[len(order) - 1 - place])
    return blocks.transpose(*turned, *range(len(order), blocks.ndim)).reshape(-1, *x.shape)


def gather_axes(x, axes, order, dim):
    return joined_along(stacked_from(x, axes, order), dim)


def reduced_to_own(blocks, axes, order):
    shape = [lax.axis_size(a) for a in axes]
    blocks = blocks.reshape(*shape, *blocks.shape[1:])
    blocks = blocks.transpose(*order, *range(len(axes), blocks.ndim))
    blocks = blocks.reshape(-1, *blocks.shape[len(axes) :])
    for k in order:
        blocks = lax.psum_scatter(blocks, axes[k], scatter_dimension=0, tiled=True)
    return blocks[0]


def in_blocks(x, dim, peers):
    before, after = (x.shape[:dim], x.shape[dim + 1 :])
    return jnp.moveaxis(x.reshape(*before, peers, -1, *after), dim, 0)


def sum_by_axis(x, axes, order, dim):
    peers = lax.axis_size(axes)
    return reduced_to_own(in_blocks(x, dim, peers), axes, order)


def by_axis(x, axes):
    for axis in axes:
        x = lax.psum(x, axis)
    return x


def contract(left, right):
    return lax.dot_general(
        left, right, (((1,), (1,)), ((), ())), preferred_element_type=jnp.float32
    )


def contract_rows(left, right):
    return lax.dot_general(
        left, right, (((0,), (0,)), ((), ())), preferred_element_type=jnp.float32
    )


def forward(inputs, core_bf, head_bf):
    width = inputs.shape[-1]
    pre_one = contract(inputs, core_bf[:, :width])
    first_act = jax.nn.relu(pre_one)
    first_bf = first_act.astype(jnp.bfloat16)
    pre_two = contract(first_bf, core_bf[:, width:])
    second_act = jax.nn.relu(pre_two) + first_act
    second_bf = second_act.astype(jnp.bfloat16)
    network_outputs = contract(second_bf, head_bf)
    return (network_outputs, pre_one, first_bf, pre_two, second_bf)


def importance_trace_gradients(
    network_outputs, bootstrap_value, actions, done, rewards, behaviour, scale_factor
):
    action_count = network_outputs.shape[-1] - 1
    logits = network_outputs[..., :action_count]
    values = network_outputs[..., action_count]
    totals = jnp.sum(jnp.exp(logits), -1)
    logp = logits - jnp.log(totals)[..., None]
    probs = jnp.exp(logp)
    chosen = (actions[..., None] == jnp.arange(action_count, dtype=jnp.int32)).astype(jnp.float32)
    logp_act = jnp.sum(logp * chosen, -1)
    ratio = jnp.minimum(1.0, jnp.exp(logp_act - behaviour))
    discount = gamma_rate * (1.0 - done.astype(jnp.float32))
    next_values = jnp.concatenate([values[:, 1:], bootstrap_value[:, None]], 1)
    deltas = ratio * (rewards + discount * next_values - values)

    def backstep(carry, item):
        delta, factor = item
        carry = delta + factor * carry
        return (carry, carry)

    start = jnp.zeros((values.shape[0],), jnp.float32)
    final_carry, corrections = lax.scan(
        backstep, start, (deltas.T, (discount * ratio).T), reverse=True
    )
    targets = values + corrections.T
    next_targets = jnp.concatenate([targets[:, 1:], bootstrap_value[:, None]], 1)
    advantage = ratio * (rewards + discount * next_targets - values)
    entropy = -jnp.sum(probs * logp, -1)
    grad_logits = scale_factor * (
        -advantage[..., None] * (chosen - probs)
        + entropy_cost * probs * (logp + entropy[..., None])
    )
    grad_value = scale_factor * (-baseline_cost * (targets - values))
    return jnp.concatenate([grad_logits, grad_value[..., None]], -1)


def adam_step(master, moment, second, grad, rate):
    moment = beta_first * moment + (1.0 - beta_first) * grad
    second = beta_second * second + (1.0 - beta_second) * grad * grad
    master = master - rate * moment / (jnp.sqrt(second) + adam_eps)
    return (master, moment, second)


def per_device(
    learn_obs,
    own_obs,
    opp_obs,
    opponent,
    actions,
    done,
    rewards,
    behaviour,
    core_master,
    core_mom,
    core_vel,
    head_master,
    head_mom,
    head_vel,
    rates,
):
    environment_total, rollout_length, width = (
        learn_obs.shape[1],
        learn_obs.shape[2],
        learn_obs.shape[3],
    )
    action_count = head_master.shape[1] - 1
    agent_count = lax.axis_size("agent")
    slots = min(environment_total, BLOCK // agent_count)
    scale_factor = 1.0 / rollout_length
    core_bf = gather_axes(core_master.astype(jnp.bfloat16), DP, (0, 1), 1)[0]
    head_bf = head_master[0].astype(jnp.bfloat16)
    own_out = forward(own_obs[0], core_bf, head_bf)[0]
    ids = opponent[0, :, 0]
    earlier = (ids[None, :] == ids[:, None]) & jnp.tril(jnp.ones((ids.shape[0],) * 2, bool), -1)
    ranks = jnp.sum(earlier.astype(jnp.int32), 1)
    position = ids * slots + ranks
    placing = (
        position[None, :] == jnp.arange(agent_count * slots, dtype=jnp.int32)[:, None]
    ).astype(jnp.bfloat16)
    outgoing = jnp.dot(placing, opp_obs[0], preferred_element_type=jnp.float32).astype(jnp.bfloat16)
    outgoing = outgoing.reshape(agent_count, slots, width)
    incoming = lax.all_to_all(outgoing, "agent", split_axis=0, concat_axis=0, tiled=True)
    count = incoming.shape[1]
    played = forward(incoming.reshape(agent_count * count, width), core_bf, head_bf)[0][
        :, :action_count
    ]
    played = played.astype(jnp.bfloat16).reshape(agent_count, count, action_count)
    returned = lax.all_to_all(played, "agent", split_axis=0, concat_axis=0, tiled=True)
    opp_logits = returned.reshape(agent_count * slots, action_count)[position]
    rows = learn_obs[0].reshape(environment_total * rollout_length, width)
    network_outputs, pre_one, first_bf, pre_two, second_bf = forward(rows, core_bf, head_bf)
    output_gradient = importance_trace_gradients(
        network_outputs.reshape(environment_total, rollout_length, action_count + 1),
        own_out[:, action_count],
        actions[0],
        done[0],
        rewards[0],
        behaviour[0],
        scale_factor,
    )
    grad_bf = output_gradient.reshape(environment_total * rollout_length, action_count + 1).astype(
        jnp.bfloat16
    )
    head_grad = contract_rows(grad_bf, second_bf)
    grad_second = jnp.dot(grad_bf, head_bf, preferred_element_type=jnp.float32)
    grad_pre_two = jnp.where(pre_two > 0, grad_second, 0.0).astype(jnp.bfloat16)
    grad_first = grad_second + jnp.dot(
        grad_pre_two, core_bf[:, width:], preferred_element_type=jnp.float32
    )
    grad_pre_one = jnp.where(pre_one > 0, grad_first, 0.0).astype(jnp.bfloat16)
    core_grad = sum_by_axis(
        jnp.concatenate(
            [contract_rows(grad_pre_one, rows), contract_rows(grad_pre_two, first_bf)], 1
        ).astype(jnp.bfloat16),
        DP,
        (1, 0),
        0,
    ).astype(jnp.float32)
    head_total = by_axis(head_grad, DP)
    rate = rates[0]
    new_core, new_core_mom, new_core_vel = adam_step(
        core_master[0], core_mom[0], core_vel[0], core_grad, rate
    )
    new_head, new_head_mom, new_head_vel = adam_step(
        head_master[0], head_mom[0], head_vel[0], head_total, rate
    )
    return (
        own_out[:, :action_count][None],
        opp_logits[None],
        new_core[None],
        new_core_mom[None],
        new_core_vel[None],
        new_head[None],
        new_head_mom[None],
        new_head_vel[None],
    )


def solution(mesh):
    torus = Mesh(mesh.devices.reshape(mesh.shape["agent"], 16, 2), ("agent", "dp_0", "dp_1"))
    return jax.shard_map(
        per_device,
        mesh=torus,
        in_specs=(
            P("agent", DP, None, None),
            P("agent", DP, None),
            P("agent", DP, None),
            P("agent", DP, None),
            P("agent", DP, None),
            P("agent", DP, None),
            P("agent", DP, None),
            P("agent", DP, None),
            P("agent", DP, None),
            P("agent", DP, None),
            P("agent", DP, None),
            P("agent", None, None),
            P("agent", None, None),
            P("agent", None, None),
            P("agent"),
        ),
        out_specs=(
            P("agent", DP, None),
            P("agent", DP, None),
            P("agent", DP, None),
            P("agent", DP, None),
            P("agent", DP, None),
            P("agent", None, None),
            P("agent", None, None),
            P("agent", None, None),
        ),
        check_vma=False,
    )
```

profile of v0, /device:TPU:1, one launch (start us, length us, event | category | flops | bytes accessed | tf_op | source)
XLA Modules:
  0.0 268.0 jit_solution(14837776084978435782)
XLA Ops:
  8.3 37.6 %all-gather = bf16[16,8,3712]{2,1,0:T(8,128)(2,1)} all-gather(bf16[1,8,3712]{2,1,0:T(8,128)(2,1)S(1)} %convert_element_type.71), channel_id=2, replica_groups=mesh['agent'=16,'dp_0'=16,'dp_1'=2] {'dp_0'}, dimensions={0}, use_global_device_ids=true | all-gather | bytes 1009664 | tf_op jit(solution)/shard_map/all_gather | solution.py:26
  46.8 1.4 convert_element_type.81
  48.1 22.9 %all-gather.4.cloned.1.call-done = bf16[32,8,3712]{2,1,0:T(8,128)(2,1)} async-done(((bf16[16,8,3712]{2,1,0:T(8,128)(2,1)}), bf16[32,8,3712]{2,1,0:T(8,128)(2,1)}) %all-gather.4.cloned.1.call-update) | async-done | bytes 1900560 | tf_op jit(solution)/shard_map/all_gather | solution.py:26
  71.0 1.7 copy.180
  75.3 1.8 fusion.26
  77.1 2.6 fusion.4
  80.5 2.0 add_convert_fusion
  84.2 2.3 fusion.33
  89.7 1.3 fusion.71
  91.6 40.4 %while.17 = (s32[]{:T(128)}, f32[32]{0:T(128)}, f32[16,32]{1,0:T(8,128)}, f32[16,32]{1,0:T(8,128)}, f32[16,32]{1,0:T(8,128)}, /*index=5*/s32[]{:T(128)}, s32[]{:T(128)}, s32[]{:T(128)}) while((s32[]{:T(128)}, f32[32]{0:T(128)}, f32[16,32]{1,0:T(8,128)}, f32[16,32]{1,0:T(8,128)}, f32[16,32]{1,0:T(8,128)}, /*index=5*/s32[]{:T(128)}, ...), condition=%wide.region_4.5_spmd.clone, body=%wide.region_3.4_spmd.clone.sunk | while | flops 100 | bytes 891 | solution.py:109
  133.4 1.4 copy.188
  134.7 1.4 concatenate.38
  138.1 1.3 fusion.70
  140.2 1.9 fusion.31
  142.1 1.6 copy.189
  144.8 2.1 convolution_convert_fusion.2
  147.0 1.9 fusion.14
  148.9 1.8 copy.193
  150.7 2.1 convolution_convert_fusion
  152.9 1.4 copy.194
  155.2 2.2 fusion.3
  157.4 5.6 %all-to-all-start = ((bf16[16,8,3456]{2,1,0:T(8,128)(2,1)}), bf16[16,8,3456]{2,1,0:T(8,128)(2,1)}, u32[]{:S(2)}, u32[]{:S(2)}) async-start(bf16[16,8,3456]{2,1,0:T(8,128)(2,1)} %fusion.3), calls=%async_computation | async-start | bytes 1769472 | tf_op jit(solution)/shard_map/all_to_all | solution.py:169
  163.0 12.6 %reduce-scatter.5.cloned.1.call-done = bf16[16,8,3712]{2,1,0:T(8,128)(2,1)} async-done(((bf16[32,8,3712]{2,1,0:T(8,128)(2,1)}), bf16[16,8,3712]{2,1,0:T(8,128)(2,1)}) %reduce-scatter.5.cloned.1.call-update) | async-done | bytes 950288 | tf_op jit(solution)/shard_map/reduce_scatter | solution.py:43
  176.9 3.1 %fusion.15 = f32[128,256]{1,0:T(8,128)} fusion(bf16[256,3712]{1,0:T(8,128)(2,1)} %bitcast.156, bf16[16,8,3456]{2,1,0:T(8,128)(2,1)} %all-to-all-done), kind=kOutput, calls=%fused_computation.22 | convolution fusion | flops 226525184 | bytes 2785280 | tf_op jit(solution)/shard_map/dot_general | solution.py:64
  180.0 2.0 fusion.20
  182.0 1.4 copy.181
  183.4 5.7 %all-to-all-start.1 = ((bf16[16,8,18]{2,1,0:T(8,128)(2,1)}), bf16[16,8,18]{2,1,0:T(8,128)(2,1)}, u32[]{:S(2)}, u32[]{:S(2)}) async-start(bf16[16,8,18]{2,1,0:T(8,128)(2,1)} %bitcast.164), calls=%async_computation.1 | async-start | bytes 65536 | tf_op jit(solution)/shard_map/all_to_all | solution.py:175
  189.2 1.7 fusion.56
  190.9 45.8 %psum.14 = f32[19,256]{1,0:T(8,128)} all-reduce(f32[19,256]{1,0:T(8,128)} %fusion.56), channel_id=1, replica_groups=mesh['agent'=16,'dp_0'=16,'dp_1'=2] {'dp_0'}, use_global_device_ids=true, to_apply=%region_8.9 | all-reduce | flops 4864 | bytes 38912 | tf_op jit(solution)/shard_map/psum | solution.py:59
  236.7 17.5 %psum.15 = f32[19,256]{1,0:T(8,128)} all-reduce(f32[19,256]{1,0:T(8,128)} %psum.14), channel_id=1, replica_groups=mesh['agent'=16,'dp_0'=16,'dp_1'=2] {'dp_1'}, use_global_device_ids=true, to_apply=%region_9.10 | all-reduce | flops 4864 | bytes 38912 | tf_op jit(solution)/shard_map/psum | solution.py:59
  257.5 1.5 gather_fusion
  259.7 1.8 divide_subtract_fusion
  (96 shorter events, 62.0 us)
Async XLA Ops:
  7.2 69.9 %copy-start = (bf16[1,32,16,3456]{3,2,1,0:T(8,128)(2,1)S(1)}, bf16[1,32,16,3456]{3,2,1,0:T(8,128)(2,1)}, u32[]{:S(2)}) copy-start(bf16[1,32,16,3456]{3,2,1,0:T(8,128)(2,1)} %param.17) | copy-start | bytes 10616836
  7.2 63.8 %all-gather.4.cloned.1.call-start = ((), (), s32[]{:S(2)}) async-start(), calls=%async_computation.5 | async-start | bytes 2850816 | tf_op jit(solution)/shard_map/all_gather | solution.py:26
  46.0 129.6 %reduce-scatter.5.cloned.1.call-start = ((), (), s32[]{:S(2)}) async-start(), calls=%async_computation.4 | async-start | bytes 2850816 | tf_op jit(solution)/shard_map/reduce_scatter | solution.py:43
  46.8 37.5 %copy-start.7 = (s32[32,16]{1,0:T(8,128)}, s32[32,16]{1,0:T(8,128)S(1)}, u32[]{:S(2)}) copy-start(s32[32,16]{1,0:T(8,128)S(1)} %copy.182) | copy-start | bytes 6148
  71.0 3.0 %copy-start.12 = (bf16[1,32,3456]{2,1,0:T(8,128)(2,1)S(1)}, bf16[1,32,3456]{2,1,0:T(8,128)(2,1)}, u32[]{:S(2)}) copy-start(bf16[1,32,3456]{2,1,0:T(8,128)(2,1)} %param.18) | copy-start | bytes 663556
  72.7 1.3 copy-start.4
  77.1 6.1 %copy-start.8 = (bf16[1,19,256]{2,0,1:T(2,128)(2,1)S(1)}, bf16[1,19,256]{2,0,1:T(2,128)(2,1)}, u32[]{:S(2)}) copy-start(bf16[1,19,256]{2,0,1:T(2,128)(2,1)} %convert_element_type.81) | copy-start | bytes 29188
  79.7 0.8 copy-start.1
  82.5 0.7 copy-start.5
  143.7 3.3 %copy-start.2 = (f32[512,256]{1,0:T(8,128)S(1)}, f32[512,256]{1,0:T(8,128)}, u32[]{:S(2)}) copy-start(f32[512,256]{1,0:T(8,128)} %copy-done.1) | copy-start | bytes 1572868
  143.7 3.3 %copy-start.3 = (f32[512,256]{1,0:T(8,128)S(1)}, f32[512,256]{1,0:T(8,128)}, u32[]{:S(2)}) copy-start(f32[512,256]{1,0:T(8,128)} %get-tuple-element.223) | copy-start | bytes 1572868
  150.7 2.1 copy-start.6
  154.3 0.7 copy-start.11
  157.4 19.5 %all-to-all-start = ((bf16[16,8,3456]{2,1,0:T(8,128)(2,1)}), bf16[16,8,3456]{2,1,0:T(8,128)(2,1)}, u32[]{:S(2)}, u32[]{:S(2)}) async-start(bf16[16,8,3456]{2,1,0:T(8,128)(2,1)} %fusion.3), calls=%async_computation | async-start | bytes 1769472 | tf_op jit(solution)/shard_map/all_to_all | solution.py:169
  163.0 96.7 %reduce-scatter.7.cloned.1.call-start = ((), (), s32[]{:S(2)}) async-start(), calls=%async_computation.6 | async-start | bytes 1009664
  175.6 13.5 %copy-start.10 = (bf16[512,1]{0,1:T(2,128)(2,1)S(1)}, bf16[512,1]{0,1:T(2,128)(2,1)}, u32[]{:S(2)}) copy-start(bf16[512,1]{0,1:T(2,128)(2,1)} %concatenate.38) | copy-start | bytes 3076
  176.9 78.1 %copy-start.9 = (f32[32,19]{0,1:T(8,128)S(1)}, f32[32,19]{0,1:T(8,128)}, u32[]{:S(2)}) copy-start(f32[32,19]{0,1:T(8,128)} %fusion.26) | copy-start | bytes 7300
  183.4 74.1 %all-to-all-start.1 = ((bf16[16,8,18]{2,1,0:T(8,128)(2,1)}), bf16[16,8,18]{2,1,0:T(8,128)(2,1)}, u32[]{:S(2)}, u32[]{:S(2)}) async-start(bf16[16,8,18]{2,1,0:T(8,128)(2,1)} %bitcast.164), calls=%async_computation.1 | async-start | bytes 65536 | tf_op jit(solution)/shard_map/all_to_all | solution.py:175
Sparse Core Ops, SparseCore 0:
  46.1 24.8 all-gather.3
  154.5 21.0 reduce-scatter.4
  178.7 60.5 reduce-scatter.6
where the time goes:
time: 271 us; the launch traced here: 268 us
  blocking collectives  101 us (37%)
  local copies, waits for them, and re-layouts  46.2 us (17%)
  waiting for transfers between devices  35.5 us (13%)
  other arithmetic  35.2 us (13%)
  matrix products  24.1 us (9%)
  between operations  14.6 us (5%)
  starting transfers between devices  11.4 us (4%)
    psum x2, blocking collectives, by_axis(): x = lax.psum(x, axis)  63.3 us
    all_gather x1, blocking collectives, stacked_from(): blocks = lax.all_gather(blocks, axes[k], axis=0, tiled=True)  37.6 us
    all_gather x1, waiting for transfers between devices, stacked_from(): blocks = lax.all_gather(blocks, axes[k], axis=0, tiled=True)  22.9 us
    dynamic_update_slice x16, local copies, waits for them, and re-layouts, importance_trace_gradients(): lax.scan(backstep, start, (deltas.T, (discount * ratio).T), reverse=True)  20.6 us
    add x16, other arithmetic, backstep(): carry = delta + factor * carry  19.8 us
    dot_general x7, matrix products, contract(): lax.dot_general(left, right, (((1,), (1,)), ((), ())), preferred_element_...  13 us
    reduce_scatter x1, waiting for transfers between devices, reduced_to_own(): blocks = lax.psum_scatter(blocks, axes[k], scatter_dimension=0, tiled=True)  12.6 us
    unnamed x32, local copies, waits for them, and re-layouts  7.75 us
  transfers between devices with their start and end apart: 5, of which 2 were waited for; matrix products, arithmetic and copies ran while one was open for 7% of the time, Pallas kernels for 0%

commit v1 on v0

--- a/solution.py
+++ b/solution.py
@@ -56,7 +56,7 @@
 
 def by_axis(x, axes):
     for axis in axes:
-        x = lax.psum(x, axis)
+        x = jnp.sum(lax.all_gather(x, axis), axis=0)
     return x
 
 

time: 271 us -> 258 us (0.952)
  the two profiles are of different devices: /device:TPU:1 before, /device:TPU:2 now
where the time goes in v1:
time: 258 us; the launch traced here: 256 us
  blocking collectives  82 us (32%)
  local copies, waits for them, and re-layouts  42.3 us (16%)
  waiting for transfers between devices  41 us (16%)
  other arithmetic  39.8 us (15%)
  matrix products  22.2 us (9%)
  between operations  14.5 us (6%)
  starting transfers between devices  14 us (5%)
    all_gather x1, blocking collectives, stacked_from(): blocks = lax.all_gather(blocks, axes[k], axis=0, tiled=True)  43.3 us
    all_gather x2, blocking collectives, by_axis(): x = jnp.sum(lax.all_gather(x, axis), axis=0)  38.7 us
    dynamic_update_slice x16, local copies, waits for them, and re-layouts, importance_trace_gradients(): lax.scan(backstep, start, (deltas.T, (discount * ratio).T), reverse=True)  20.6 us
    add x16, other arithmetic, backstep(): carry = delta + factor * carry  20.6 us
    all_gather x1, waiting for transfers between devices, stacked_from(): blocks = lax.all_gather(blocks, axes[k], axis=0, tiled=True)  14.9 us
    unnamed x4, waiting for transfers between devices  13.7 us
    dot_general x7, matrix products, contract(): lax.dot_general(left, right, (((1,), (1,)), ((), ())), preferred_element_...  11.6 us
    reduce_scatter x1, waiting for transfers between devices, reduced_to_own(): blocks = lax.psum_scatter(blocks, axes[k], scatter_dimension=0, tiled=True)  11 us
  transfers between devices with their start and end apart: 5, of which 4 were waited for; matrix products, arithmetic and copies ran while one was open for 8% of the time, Pallas kernels for 0%

profile of v1, /device:TPU:2, one launch (start us, length us, event | category | flops | bytes accessed | tf_op | source)
XLA Modules:
  0.0 255.8 jit_solution(6050916328476935447)
XLA Ops:
  8.3 43.3 %all-gather = bf16[16,8,3712]{2,1,0:T(8,128)(2,1)} all-gather(bf16[1,8,3712]{2,1,0:T(8,128)(2,1)S(1)} %convert_element_type.70), channel_id=2, replica_groups=mesh['agent'=16,'dp_0'=16,'dp_1'=2] {'dp_0'}, dimensions={0}, use_global_device_ids=true | all-gather | bytes 1009664 | tf_op jit(solution)/shard_map/all_gather | solution.py:26
  51.7 1.3 convert_element_type.73
  53.8 14.9 %all-gather.8.cloned.1.call-done = bf16[32,8,3712]{2,1,0:T(8,128)(2,1)} async-done(((bf16[16,8,3712]{2,1,0:T(8,128)(2,1)}), bf16[32,8,3712]{2,1,0:T(8,128)(2,1)}) %all-gather.8.cloned.1.call-update) | async-done | bytes 1900560 | tf_op jit(solution)/shard_map/all_gather | solution.py:26
  68.7 1.7 copy.155
  74.8 1.8 fusion.26
  78.6 2.3 fusion.33
  86.0 41.2 %while.17 = (s32[]{:T(128)}, f32[32]{0:T(128)}, f32[16,32]{1,0:T(8,128)}, f32[16,32]{1,0:T(8,128)}, f32[16,32]{1,0:T(8,128)}, /*index=5*/s32[]{:T(128)}, s32[]{:T(128)}, s32[]{:T(128)}) while((s32[]{:T(128)}, f32[32]{0:T(128)}, f32[16,32]{1,0:T(8,128)}, f32[16,32]{1,0:T(8,128)}, f32[16,32]{1,0:T(8,128)}, /*index=5*/s32[]{:T(128)}, ...), condition=%wide.region_4.5_spmd.clone, body=%wide.region_3.4_spmd.clone.sunk | while | flops 100 | bytes 891 | solution.py:109
  128.5 1.4 copy.163
  129.9 1.4 concatenate.38
  135.4 1.9 fusion.31
  137.3 1.6 copy.164
  140.0 2.1 convolution_convert_fusion.2
  142.2 1.9 fusion.14
  144.0 1.8 copy.168
  145.8 2.1 convolution_convert_fusion
  148.1 1.4 copy.169
  150.3 2.2 fusion.3
  152.5 7.3 %all-to-all-start = ((bf16[16,8,3456]{2,1,0:T(8,128)(2,1)}), bf16[16,8,3456]{2,1,0:T(8,128)(2,1)}, u32[]{:S(2)}, u32[]{:S(2)}) async-start(bf16[16,8,3456]{2,1,0:T(8,128)(2,1)} %fusion.3), calls=%async_computation | async-start | bytes 1769472 | tf_op jit(solution)/shard_map/all_to_all | solution.py:169
  159.9 11.0 %reduce-scatter.5.cloned.1.call-done = bf16[16,8,3712]{2,1,0:T(8,128)(2,1)} async-done(((bf16[32,8,3712]{2,1,0:T(8,128)(2,1)}), bf16[16,8,3712]{2,1,0:T(8,128)(2,1)}) %reduce-scatter.5.cloned.1.call-update) | async-done | bytes 950288 | tf_op jit(solution)/shard_map/reduce_scatter | solution.py:43
  172.2 1.4 all-to-all-done
  173.6 3.1 %fusion.15 = f32[128,256]{1,0:T(8,128)} fusion(bf16[256,3712]{1,0:T(8,128)(2,1)} %bitcast.140, bf16[16,8,3456]{2,1,0:T(8,128)(2,1)} %all-to-all-done), kind=kOutput, calls=%fused_computation.22 | convolution fusion | flops 226525184 | bytes 2785280 | tf_op jit(solution)/shard_map/dot_general | solution.py:64
  176.7 2.0 fusion.20
  178.7 1.4 copy.156
  180.1 6.6 %all-to-all-start.1 = ((bf16[16,8,18]{2,1,0:T(8,128)(2,1)}), bf16[16,8,18]{2,1,0:T(8,128)(2,1)}, u32[]{:S(2)}, u32[]{:S(2)}) async-start(bf16[16,8,18]{2,1,0:T(8,128)(2,1)} %bitcast.148), calls=%async_computation.1 | async-start | bytes 65536 | tf_op jit(solution)/shard_map/all_to_all | solution.py:175
  187.8 35.5 %all-gather.4 = f32[16,19,256]{2,1,0:T(8,128)} all-gather(f32[1,19,256]{2,1,0:T(8,128)S(1)} %convolution_bitcast_fusion), channel_id=4, replica_groups=mesh['agent'=16,'dp_0'=16,'dp_1'=2] {'dp_0'}, dimensions={0}, use_global_device_ids=true | all-gather | bytes 330752 | tf_op jit(solution)/shard_map/all_gather | solution.py:59
  223.3 1.6 reduce_sum.66
  225.0 3.2 %all-gather.5 = f32[2,19,256]{2,1,0:T(8,128)} all-gather(f32[1,19,256]{2,1,0:T(8,128)} %bitcast.149), channel_id=5, replica_groups=mesh['agent'=16,'dp_0'=16,'dp_1'=2] {'dp_1'}, dimensions={0}, use_global_device_ids=true | all-gather | bytes 58368 | tf_op jit(solution)/shard_map/all_gather | solution.py:59
  228.1 1.4 reduce_sum.67
  229.5 1.5 divide_subtract_fusion.1
  231.7 1.5 gather_fusion
  233.8 13.6 %reduce-scatter.7.cloned.1.call-done = bf16[1,8,3712]{2,1,0:T(8,128)(2,1)} async-done(((bf16[16,8,3712]{2,1,0:T(8,128)(2,1)}), bf16[1,8,3712]{2,1,0:T(8,128)(2,1)}) %reduce-scatter.7.cloned.1.call-update) | async-done | bytes 59408
  247.4 1.8 divide_subtract_fusion
  (91 shorter events, 65.2 us)
Async XLA Ops:
  7.2 64.5 %copy-start = (bf16[1,32,16,3456]{3,2,1,0:T(8,128)(2,1)S(1)}, bf16[1,32,16,3456]{3,2,1,0:T(8,128)(2,1)}, u32[]{:S(2)}) copy-start(bf16[1,32,16,3456]{3,2,1,0:T(8,128)(2,1)} %param.17) | copy-start | bytes 10616836
  7.2 61.5 %all-gather.8.cloned.1.call-start = ((), (), s32[]{:S(2)}) async-start(), calls=%async_computation.5 | async-start | bytes 2850816 | tf_op jit(solution)/shard_map/all_gather | solution.py:26
  51.6 119.3 %reduce-scatter.5.cloned.1.call-start = ((), (), s32[]{:S(2)}) async-start(), calls=%async_computation.4 | async-start | bytes 2850816 | tf_op jit(solution)/shard_map/reduce_scatter | solution.py:43
  53.8 24.8 %copy-start.6 = (s32[32,16]{1,0:T(8,128)}, s32[32,16]{1,0:T(8,128)S(1)}, u32[]{:S(2)}) copy-start(s32[32,16]{1,0:T(8,128)S(1)} %copy.157) | copy-start | bytes 6148
  68.7 1.7 copy-start.10
  70.4 2.4 copy-start.4
  72.8 0.8 copy-start.1
  138.9 3.3 %copy-start.2 = (f32[512,256]{1,0:T(8,128)S(1)}, f32[512,256]{1,0:T(8,128)}, u32[]{:S(2)}) copy-start(f32[512,256]{1,0:T(8,128)} %copy-done.1) | copy-start | bytes 1572868
  138.9 3.3 %copy-start.3 = (f32[512,256]{1,0:T(8,128)S(1)}, f32[512,256]{1,0:T(8,128)}, u32[]{:S(2)}) copy-start(f32[512,256]{1,0:T(8,128)} %get-tuple-element.223) | copy-start | bytes 1572868
  145.8 2.1 copy-start.5
  149.5 0.7 copy-start.9
  152.5 21.1 %all-to-all-start = ((bf16[16,8,3456]{2,1,0:T(8,128)(2,1)}), bf16[16,8,3456]{2,1,0:T(8,128)(2,1)}, u32[]{:S(2)}, u32[]{:S(2)}) async-start(bf16[16,8,3456]{2,1,0:T(8,128)(2,1)} %fusion.3), calls=%async_computation | async-start | bytes 1769472 | tf_op jit(solution)/shard_map/all_to_all | solution.py:169
  159.8 87.6 %reduce-scatter.7.cloned.1.call-start = ((), (), s32[]{:S(2)}) async-start(), calls=%async_computation.6 | async-start | bytes 1009664
  170.9 15.8 %copy-start.8 = (bf16[512,1]{0,1:T(2,128)(2,1)S(1)}, bf16[512,1]{0,1:T(2,128)(2,1)}, u32[]{:S(2)}) copy-start(bf16[512,1]{0,1:T(2,128)(2,1)} %concatenate.38) | copy-start | bytes 3076
  172.2 58.9 %copy-start.7 = (f32[32,19]{0,1:T(8,128)S(1)}, f32[32,19]{0,1:T(8,128)}, u32[]{:S(2)}) copy-start(f32[32,19]{0,1:T(8,128)} %fusion.26) | copy-start | bytes 7300
  180.1 51.6 %all-to-all-start.1 = ((bf16[16,8,18]{2,1,0:T(8,128)(2,1)}), bf16[16,8,18]{2,1,0:T(8,128)(2,1)}, u32[]{:S(2)}, u32[]{:S(2)}) async-start(bf16[16,8,18]{2,1,0:T(8,128)(2,1)} %bitcast.148), calls=%async_computation.1 | async-start | bytes 65536 | tf_op jit(solution)/shard_map/all_to_all | solution.py:175
Sparse Core Ops, SparseCore 0:
  51.8 16.9 all-gather.7
  149.6 21.2 reduce-scatter.4
  174.0 73.4 reduce-scatter.6
